TPU v7x, 32 devices: a whole 2x2x4 slice. The times are simulated.
32 devices in a mesh: row: 2 (over core), blk: 16 (over z, y, x).
Axes of the slice: x: 2, y: 2, z: 4, core: 2. Of those that a mesh axis runs over, the one named last changes fastest.
Arguments:
- flow_state: float32 [2, 16, 6, 16, 64, 256], P('row', 'blk'), may hold values from -6 to 6
- forcing: float32 [2, 16, 6, 16, 64, 256], P('row', 'blk'), may hold values from -6 to 6
- stiffness: float32 [2, 16, 16, 64, 256], P('row', 'blk'), may hold values from 7 to 14
- advection: float32 [2, 16, 6, 6], P('row', 'blk'), may hold values from -4 to 4
- line_inverse: float32 [2, 16, 96, 96], P('row', 'blk')
- margin_rows: int32 [2, 16, 64, 4], P('row', 'blk'), may hold values from 0 to 67, as said below
- margin_weights: float32 [2, 16, 64, 4], P('row', 'blk'), may hold values from 0 to 1, as said below
- partner_bit: int32 [2, 16], P('row', 'blk'), may hold values from 0 to 2, as said below
- turn_code: int32 [2, 16], P('row', 'blk'), may hold values from 0 to 3, as said below
Outputs:
- final_state: float32 [2, 16, 6, 16, 64, 256], P('row', 'blk')
Inputs may be any that keep to these rules, and one draw needn't show every extreme that they name: Within a blade row, blocks 8g to 8g+7 share one value, so that b and b XOR 2**partner_bit[r,b] name each other. `turn_code`: A block and its face partner carry the same code. `margin_rows`: row j of a block reads window rows j to j + 4 only. `margin_weights`: the first 1 to 4 slots of a row carry positive weights summing to one, the others zero.
All inputs are finite; a program needn't handle non-finite values.
Results may differ from a plain program's by a relative error of at most 0.0001.
Values sent between devices are 32-bit elements; how exact they have to be, the bound alone decides.
A program may use at most 128 MiB of HBM per device.

v0:
```python
import functools

import jax
import jax.numpy as jnp
from jax import lax
from jax.experimental import pallas as pl
from jax.experimental.pallas import tpu as pltpu
from jax.sharding import PartitionSpec as P

HW = 2
SWEEPS = 3
BITS = 3
CHUNK = 8
MESH = pl.DeviceIdType.MESH
EXACT = lax.Precision.HIGHEST


def line_matrix(inverse_ref, jacobian_ref, rotor, nv, ni):
    order = nv * ni
    width = 2 * order + 16
    row = lax.broadcasted_iota(jnp.int32, (order, width), 0)
    col = lax.broadcasted_iota(jnp.int32, (order, width), 1)
    v, i = row // ni, row % ni
    identity = col == row
    in_state = (col >= order) & (col < 2 * order)
    cs = col - order
    w, ic = cs // ni, cs % ni
    ghost = cs - order
    is_ghost = col >= 2 * order
    rotor_m = jnp.broadcast_to(rotor, (order, width))
    top, bottom = i == ni - 1, i == 0
    stator_m = jnp.logical_not(rotor_m)
    up = (in_state & ((ic == i + 1) | (stator_m & top & (ic == ni - 1)))) | (is_ghost & rotor_m & top)
    down = (in_state & ((ic == i - 1) | (rotor_m & bottom & (ic == 0)))) | (
        is_ghost & stator_m & bottom
    )
    upf = jnp.where(up, 1.0, 0.0)
    downf = jnp.where(down, 1.0, 0.0)
    wv = jnp.where(is_ghost, ghost, w)
    coupling = jnp.zeros((order, width), jnp.float32)
    for a in range(nv):
        for b in range(nv):
            coupling = jnp.where((v == a) & (wv == b), jacobian_ref[a, b], coupling)
    same = jnp.where(v == wv, 1.0, 0.0)
    m = jnp.where(identity, 1.0, 0.0) + same * (upf + downf) - 0.5 * coupling * (upf - downf)
    return jnp.dot(inverse_ref[...], m, precision=EXACT, preferred_element_type=jnp.float32)


def kernel(
    nblk,
    nv,
    ni,
    x_hbm,
    f_hbm,
    d_hbm,
    jac,
    inverse,
    mrows,
    mweights,
    pbit,
    tcode,
    out_hbm,
    S,
    F,
    D,
    xs,
    fs,
    ds,
    recv,
    win,
    plane,
    wcat,
    turn_i,
    turn_k,
    coef,
    in_sem,
    out_sem,
    face_send,
    face_recv,
    sis_send,
    sis_recv,
    edge_send,
    edge_recv,
):
    order = nv * ni
    nj, nk = x_hbm.shape[1], x_hbm.shape[2]
    nch = nj // CHUNK
    r = lax.axis_index("row")
    b = lax.axis_index("blk")
    rotor = r == 0
    other = 1 - r
    nxt = lax.rem(b + 1, nblk)
    prv = lax.rem(b + nblk - 1, nblk)
    partners = []
    for bit in range(BITS):
        s = 1 << bit
        partners.append(b + s * (1 - 2 * ((b // s) % 2)))

    def load(which, src, dst, c):
        rows = pl.ds(pl.multiple_of(c * CHUNK, CHUNK), CHUNK)
        return pltpu.make_async_copy(src.at[:, rows, :], dst.at[:, rows, :], in_sem.at[which, c])

    def store(c):
        rows = pl.ds(pl.multiple_of(c * CHUNK, CHUNK), CHUNK)
        return pltpu.make_async_copy(xs.at[:, rows, :], out_hbm.at[:, rows, :], out_sem.at[c])

    for c in [0, nch - 1] + list(range(1, nch - 1)):
        load(0, x_hbm, xs, c).start()
    for c in list(range(2, nch - 2)) + [1, nch - 2, 0, nch - 1]:
        load(1, f_hbm, fs, c).start()
        load(2, d_hbm, ds, c).start()

    barrier = pltpu.get_barrier_semaphore()
    friends = [(other, b), (other, prv), (other, nxt)] + [(r, p) for p in partners]
    for friend in friends:
        pl.semaphore_signal(barrier, inc=1, device_id=friend, device_id_type=MESH)

    wfull = line_matrix(inverse, jac, rotor, nv, ni)
    whi = wfull.astype(jnp.bfloat16)
    wlo = (wfull - whi.astype(jnp.float32)).astype(jnp.bfloat16)
    wcat[0:order, :] = whi
    wcat[order : 2 * order, :] = wlo
    code = tcode[0, 0]
    ra = lax.broadcasted_iota(jnp.int32, (order, order), 0)
    ca = lax.broadcasted_iota(jnp.int32, (order, order), 1)
    turned = ra // ni * ni + (ni - 1 - ra % ni)
    turn_i[...] = jnp.where(ca == jnp.where(code % 2 == 1, turned, ra), 1.0, 0.0)
    rk = lax.broadcasted_iota(jnp.int32, (nk, nk), 0)
    ck = lax.broadcasted_iota(jnp.int32, (nk, nk), 1)
    turn_k[...] = jnp.where(ck == jnp.where(code // 2 == 1, nk - 1 - rk, rk), 1.0, 0.0)

    def coefs(j, carry):
        for d in range(2 * HW + 1):
            total = jnp.float32(0.0)
            for o in range(mrows.shape[1]):
                total = total + jnp.where(mrows[j, o] == j + d, mweights[j, o], 0.0)
            coef[j, d] = total
        return carry

    lax.fori_loop(0, nj, coefs, 0)
    plane[...] = jnp.zeros_like(plane)

    def face(e, bit, f):
        return pltpu.make_async_remote_copy(
            src_ref=S.at[e % 2, 1 if f == 0 else nj],
            dst_ref=recv.at[e, bit, f],
            send_sem=face_send.at[e, bit, f],
            recv_sem=face_recv.at[e, bit, f],
            device_id=(r, partners[bit]),
            device_id_type=MESH,
        )

    def sister(e, c):
        return pltpu.make_async_remote_copy(
            src_ref=plane.at[e, pl.ds(c * CHUNK, CHUNK)],
            dst_ref=win.at[e, pl.ds(HW + c * CHUNK, CHUNK)],
            send_sem=sis_send.at[e, c],
            recv_sem=sis_recv.at[e, c],
            device_id=(other, b),
            device_id_type=MESH,
        )

    def edge(e, f):
        return pltpu.make_async_remote_copy(
            src_ref=plane.at[e, pl.ds(nj - HW if f == 0 else 0, HW)],
            dst_ref=win.at[e, pl.ds(0 if f == 0 else nj + HW, HW)],
            send_sem=edge_send.at[e, f],
            recv_sem=edge_recv.at[e, f],
            device_id=(other, nxt if f == 0 else prv),
            device_id_type=MESH,
        )

    def put_plane(e, j, new):
        for v in range(nv):
            last = new[v * ni + ni - 1 : v * ni + ni]
            first = new[v * ni : v * ni + 1]
            plane[e, j, v : v + 1, :] = jnp.where(rotor, last, first)

    def send_ends(e, f):
        for bit in range(BITS):
            face(e, bit, f).start()
        edge(e, 1 - f).start()

    def take_state(c):
        load(0, x_hbm, xs, c).wait()
        j0 = pl.multiple_of(c * CHUNK, CHUNK)

        def group(g, carry):
            gr = pl.ds(pl.multiple_of(g * 8, 8), 8)
            S[0, pl.ds(j0 + 1, CHUNK), gr, :] = jnp.swapaxes(xs[gr, pl.ds(j0, CHUNK), :], 0, 1)
            return carry

        lax.fori_loop(0, order // 8, group, 0)

        def planes(jj, carry):
            put_plane(0, j0 + jj, S[0, j0 + jj + 1])
            return carry

        lax.fori_loop(0, CHUNK, planes, 0)

    def take_rest(c):
        load(1, f_hbm, fs, c).wait()
        load(2, d_hbm, ds, c).wait()
        j0 = pl.multiple_of(c * CHUNK, CHUNK)

        def group(g, carry):
            gr = pl.ds(pl.multiple_of(g * 8, 8), 8)
            F[pl.ds(j0, CHUNK), gr, :] = jnp.swapaxes(fs[gr, pl.ds(j0, CHUNK), :], 0, 1)
            return carry

        lax.fori_loop(0, order // 8, group, 0)
        for g in range(ni // 8):
            gr = pl.ds(g * 8, 8)
            D[pl.ds(j0, CHUNK), gr, :] = jnp.swapaxes(ds[gr, pl.ds(j0, CHUNK), :], 0, 1)

    take_state(0)
    pl.semaphore_wait(barrier, len(friends))
    sister(0, 0).start()
    send_ends(0, 0)
    take_state(nch - 1)
    sister(0, nch - 1).start()
    send_ends(0, 1)

    def middle(c, carry):
        take_state(c)
        sister(0, c).start()
        return carry

    lax.fori_loop(1, nch - 1, middle, 0)

    lane = lax.broadcasted_iota(jnp.int32, (order, nk), 1)

    def sweep_row(e, j):
        src, dst = e % 2, (e + 1) % 2
        x = S[src, j + 1]
        below = jnp.where(lane == 0, 0.0, pltpu.roll(x, 1, 1))
        above = jnp.where(lane == nk - 1, 0.0, pltpu.roll(x, nk - 1, 1))
        diag = D[j]
        diag = jnp.concatenate([diag] * nv, axis=0)
        near = (S[src, j] + S[src, j + 2]) + (below + above)
        res = F[j] - diag * x + near
        g = coef[j, 0] * win[e, j]
        for d in range(1, 2 * HW + 1):
            g = g + coef[j, d] * win[e, j + d]
        full = jnp.concatenate([res, x, g, jnp.zeros_like(g)], axis=0)
        hi = full.astype(jnp.bfloat16)
        lo = (full - hi.astype(jnp.float32)).astype(jnp.bfloat16)
        o = jnp.dot(wcat[...], hi, preferred_element_type=jnp.float32)
        o2 = jnp.dot(wcat[0:order, :], lo, preferred_element_type=jnp.float32)
        new = x + (o[0:order] + (o[order:] + o2))
        S[dst, j + 1] = new
        if e + 1 < SWEEPS:
            put_plane(e + 1, j, new)

    def do_chunk(e, c):
        if e == 0:
            take_rest(c)
        j0 = c * CHUNK

        def rows(t, carry):
            sweep_row(e, j0 + 2 * t)
            sweep_row(e, j0 + 2 * t + 1)
            return carry

        lax.fori_loop(0, CHUNK // 2, rows, 0)
        if e + 1 < SWEEPS:
            sister(e + 1, c).start()
        else:
            j0 = pl.multiple_of(j0, CHUNK)

            def group(g, carry):
                gr = pl.ds(pl.multiple_of(g * 8, 8), 8)
                xs[gr, pl.ds(j0, CHUNK), :] = jnp.swapaxes(
                    S[(e + 1) % 2, pl.ds(j0 + 1, CHUNK), gr, :], 0, 1
                )
                return carry

            lax.fori_loop(0, order // 8, group, 0)
            store(c).start()

    def ghost_row(e, f):
        picked = recv[e, 0, 1 - f]
        for bit in range(1, BITS):
            picked = jnp.where(pbit[0, 0] == bit, recv[e, bit, 1 - f], picked)
        picked = jnp.dot(picked, turn_k[...], precision=EXACT, preferred_element_type=jnp.float32)
        picked = jnp.dot(turn_i[...], picked, precision=EXACT, preferred_element_type=jnp.float32)
        S[e % 2, 0 if f == 0 else nj + 1] = picked

    for e in range(SWEEPS):
        sister(e, 1).wait_recv()
        sister(e, 2).wait_recv()

        def inner(c, carry):
            sister(e, c + 1).wait_recv()
            do_chunk(e, c)
            return carry

        lax.fori_loop(2, nch - 2, inner, 0)
        sister(e, 0).wait_recv()
        do_chunk(e, 1)
        sister(e, nch - 1).wait_recv()
        do_chunk(e, nch - 2)
        for bit in range(BITS):
            for f in range(2):
                face(e, bit, f).wait()
        for f in range(2):
            edge(e, f).wait()
            ghost_row(e, f)
        do_chunk(e, 0)
        if e + 1 < SWEEPS:
            send_ends(e + 1, 0)
        do_chunk(e, nch - 1)
        if e + 1 < SWEEPS:
            send_ends(e + 1, 1)

        def sent(c, carry):
            sister(e, c).wait_send()
            return carry

        lax.fori_loop(0, nch, sent, 0)

    def finish(c, carry):
        store(c).wait()
        return carry

    lax.fori_loop(0, nch, finish, 0)


def body(nblk, state, forcing, stiffness, advection, inverse, mrows, mweights, pbit, tcode):
    _, _, nv, ni, nj, nk = state.shape
    order = nv * ni
    nch = nj // CHUNK
    f32 = jnp.float32
    anywhere = pl.BlockSpec(memory_space=pl.ANY)
    smem = pl.BlockSpec(memory_space=pltpu.SMEM)
    vmem = pl.BlockSpec(memory_space=pltpu.VMEM)
    dma = pltpu.SemaphoreType.DMA
    out = pl.pallas_call(
        functools.partial(kernel, nblk, nv, ni),
        out_shape=jax.ShapeDtypeStruct((order, nj, nk), f32),
        in_specs=[anywhere] * 3 + [smem, vmem, smem, smem, smem, smem],
        out_specs=anywhere,
        scratch_shapes=[
            pltpu.VMEM((2, nj + 2, order, nk), f32),
            pltpu.VMEM((nj, order, nk), f32),
            pltpu.VMEM((nj, ni, nk), f32),
            pltpu.VMEM((order, nj, nk), f32),
            pltpu.VMEM((order, nj, nk), f32),
            pltpu.VMEM((ni, nj, nk), f32),
            pltpu.VMEM((SWEEPS, BITS, 2, order, nk), f32),
            pltpu.VMEM((SWEEPS, nj + 2 * HW, 8, nk), f32),
            pltpu.VMEM((SWEEPS, nj, 8, nk), f32),
            pltpu.VMEM((2 * order, 2 * order + 16), jnp.bfloat16),
            pltpu.VMEM((order, order), f32),
            pltpu.VMEM((nk, nk), f32),
            pltpu.SMEM((nj, 2 * HW + 1), f32),
            dma((3, nch)),
            dma((nch,)),
            dma((SWEEPS, BITS, 2)),
            dma((SWEEPS, BITS, 2)),
            dma((SWEEPS, nch)),
            dma((SWEEPS, nch)),
            dma((SWEEPS, 2)),
            dma((SWEEPS, 2)),
        ],
        compiler_params=pltpu.CompilerParams(
            collective_id=0, has_side_effects=True, vmem_limit_bytes=56 * 1024 * 1024
        ),
        cost_estimate=pl.CostEstimate(
            flops=SWEEPS * 6 * order * (2 * order + 16) * nj * nk,
            bytes_accessed=4 * (3 * nv + 1) * ni * nj * nk,
            transcendentals=0,
        ),
    )(
        state.reshape(order, nj, nk),
        forcing.reshape(order, nj, nk),
        stiffness.reshape(ni, nj, nk),
        advection[0, 0],
        inverse[0, 0],
        mrows[0, 0],
        mweights[0, 0],
        pbit,
        tcode,
    )
    return out.reshape(state.shape)


def solution(mesh):
    return jax.shard_map(
        functools.partial(body, mesh.shape["blk"]),
        mesh=mesh,
        in_specs=(
            P("row", "blk", None, None, None, None),
            P("row", "blk", None, None, None, None),
            P("row", "blk", None, None, None),
            P("row", "blk", None, None),
            P("row", "blk", None, None),
            P("row", "blk", None, None),
            P("row", "blk", None, None),
            P("row", "blk"),
            P("row", "blk"),
        ),
        out_specs=P("row", "blk", None, None, None, None),
        check_vma=False,
    )
```

profile of v0, /device:TPU:0, one launch (start us, length us, event | category | flops | bytes accessed | tf_op | source)
XLA Modules:
  0.0 71.0 jit_solution(14263795967106977146)
XLA Ops:
  1.3 1.3 %copy.14 = f32[1,1,6,6]{3,2,1,0:T(8,128)} copy(f32[1,1,6,6]{3,1,2,0:T(1,128)} %param.12) | data formatting | bytes 288
  2.6 1.4 %copy.10 = s32[1,1,64,4]{3,2,1,0:T(8,128)} copy(s32[1,1,64,4]{2,3,1,0:T(4,128)} %param.14) | data formatting | bytes 2048 | tf_op args[5]
  4.0 1.4 %copy.11 = f32[1,1,64,4]{3,2,1,0:T(8,128)} copy(f32[1,1,64,4]{2,3,1,0:T(4,128)} %param.15) | data formatting | bytes 2048 | tf_op args[6]
  5.3 59.4 %shard_map.91 = f32[96,64,256]{2,1,0:T(8,128)} custom-call(f32[96,64,256]{2,1,0:T(8,128)} %bitcast.14, f32[96,64,256]{2,1,0:T(8,128)} %bitcast.15, f32[16,64,256]{2,1,0:T(8,128)} %bitcast.16, f32[6,6]{1,0:T(8,128)} %bitcast.13, f32[96,96]{1,0:T(8,128)} %bitcast.17, s32[64,4]{1,0:T(8,128)} %bitcast.11, f32[64,4]{1,0:T(8,128)} %bitcast.12, ...), custom_call_target="tpu_custom_call" | custom-call | flops 5888802816 | bytes 19922944 | tf_op jit(solution)/shard_map/pallas_call | solution.py:338
  64.7 6.3 %copy.18 = f32[1,1,6,16,64,256]{5,4,3,2,1,0:T(8,128)} copy(f32[1,1,6,16,64,256]{5,4,3,2,1,0:T(8,128)} %bitcast.10) | data formatting | bytes 12582912
where the time goes:
time: 71.4 us; the launch traced here: 71 us
  Pallas kernels  59.4 us (83%)
  local copies, waits for them, and re-layouts  10.3 us (14%)
  between operations  1.31 us (2%)
    pallas_call x1, Pallas kernels, body(): pl.pallas_call(functools.partial(kernel, nblk, nv, ni), out_shape=jax.Sha...  59.4 us
    unnamed x4, local copies, waits for them, and re-layouts  10.3 us

commit v1 on v0

--- a/solution.py
+++ b/solution.py
@@ -40,7 +40,7 @@
     coupling = jnp.zeros((order, width), jnp.float32)
     for a in range(nv):
         for b in range(nv):
-            coupling = jnp.where((v == a) & (wv == b), jacobian_ref[a, b], coupling)
+            coupling = jnp.where((v == a) & (wv == b), jacobian_ref[a, 0, b], coupling)
     same = jnp.where(v == wv, 1.0, 0.0)
     m = jnp.where(identity, 1.0, 0.0) + same * (upf + downf) - 0.5 * coupling * (upf - downf)
     return jnp.dot(inverse_ref[...], m, precision=EXACT, preferred_element_type=jnp.float32)
@@ -60,7 +60,8 @@
     pbit,
     tcode,
     out_hbm,
-    S,
+    S0,
+    S1,
     F,
     D,
     xs,
@@ -83,6 +84,7 @@
     edge_recv,
 ):
     order = nv * ni
+    S = (S0, S1)
     nj, nk = x_hbm.shape[1], x_hbm.shape[2]
     nch = nj // CHUNK
     r = lax.axis_index("row")
@@ -124,25 +126,27 @@
     ra = lax.broadcasted_iota(jnp.int32, (order, order), 0)
     ca = lax.broadcasted_iota(jnp.int32, (order, order), 1)
     turned = ra // ni * ni + (ni - 1 - ra % ni)
-    turn_i[...] = jnp.where(ca == jnp.where(code % 2 == 1, turned, ra), 1.0, 0.0)
+    chosen = jnp.where(code % 2 == 1, turned, ra)
+    turn_i[...] = jnp.where(ca == chosen, 1.0, 0.0).astype(jnp.bfloat16)
     rk = lax.broadcasted_iota(jnp.int32, (nk, nk), 0)
     ck = lax.broadcasted_iota(jnp.int32, (nk, nk), 1)
-    turn_k[...] = jnp.where(ck == jnp.where(code // 2 == 1, nk - 1 - rk, rk), 1.0, 0.0)
+    chosen_k = jnp.where(code // 2 == 1, nk - 1 - rk, rk)
+    turn_k[...] = jnp.where(ck == chosen_k, 1.0, 0.0).astype(jnp.bfloat16)
 
     def coefs(j, carry):
         for d in range(2 * HW + 1):
             total = jnp.float32(0.0)
-            for o in range(mrows.shape[1]):
-                total = total + jnp.where(mrows[j, o] == j + d, mweights[j, o], 0.0)
+            for o in range(mrows.shape[0]):
+                total = total + jnp.where(mrows[o, j] == j + d, mweights[o, j], 0.0)
             coef[j, d] = total
         return carry
 
-    lax.fori_loop(0, nj, coefs, 0)
+    lax.fori_loop(0, nj, coefs, 0, unroll=2)
     plane[...] = jnp.zeros_like(plane)
 
     def face(e, bit, f):
         return pltpu.make_async_remote_copy(
-            src_ref=S.at[e % 2, 1 if f == 0 else nj],
+            src_ref=S[e % 2].at[1 if f == 0 else nj],
             dst_ref=recv.at[e, bit, f],
             send_sem=face_send.at[e, bit, f],
             recv_sem=face_recv.at[e, bit, f],
@@ -187,16 +191,13 @@
 
         def group(g, carry):
             gr = pl.ds(pl.multiple_of(g * 8, 8), 8)
-            S[0, pl.ds(j0 + 1, CHUNK), gr, :] = jnp.swapaxes(xs[gr, pl.ds(j0, CHUNK), :], 0, 1)
+            S0[pl.ds(j0 + 1, CHUNK), gr, :] = jnp.swapaxes(xs[gr, pl.ds(j0, CHUNK), :], 0, 1)
             return carry
 
-        lax.fori_loop(0, order // 8, group, 0)
-
-        def planes(jj, carry):
-            put_plane(0, j0 + jj, S[0, j0 + jj + 1])
-            return carry
-
-        lax.fori_loop(0, CHUNK, planes, 0)
+        lax.fori_loop(0, order // 8, group, 0, unroll=6)
+
+        for jj in range(CHUNK):
+            put_plane(0, j0 + jj, S0[j0 + jj + 1])
 
     def take_rest(c):
         load(1, f_hbm, fs, c).wait()
@@ -208,7 +209,7 @@
             F[pl.ds(j0, CHUNK), gr, :] = jnp.swapaxes(fs[gr, pl.ds(j0, CHUNK), :], 0, 1)
             return carry
 
-        lax.fori_loop(0, order // 8, group, 0)
+        lax.fori_loop(0, order // 8, group, 0, unroll=6)
         for g in range(ni // 8):
             gr = pl.ds(g * 8, 8)
             D[pl.ds(j0, CHUNK), gr, :] = jnp.swapaxes(ds[gr, pl.ds(j0, CHUNK), :], 0, 1)
@@ -230,39 +231,39 @@
 
     lane = lax.broadcasted_iota(jnp.int32, (order, nk), 1)
 
-    def sweep_row(e, j):
-        src, dst = e % 2, (e + 1) % 2
-        x = S[src, j + 1]
+    def halves(value):
+        hi = value.astype(jnp.bfloat16)
+        return hi, (value - hi.astype(jnp.float32)).astype(jnp.bfloat16)
+
+    def right_hand(e, j):
+        src = S[e % 2]
+        x = src[j + 1]
         below = jnp.where(lane == 0, 0.0, pltpu.roll(x, 1, 1))
         above = jnp.where(lane == nk - 1, 0.0, pltpu.roll(x, nk - 1, 1))
-        diag = D[j]
-        diag = jnp.concatenate([diag] * nv, axis=0)
-        near = (S[src, j] + S[src, j + 2]) + (below + above)
+        diag = jnp.concatenate([D[j]] * nv, axis=0)
+        near = (src[j] + src[j + 2]) + (below + above)
         res = F[j] - diag * x + near
         g = coef[j, 0] * win[e, j]
         for d in range(1, 2 * HW + 1):
             g = g + coef[j, d] * win[e, j + d]
-        full = jnp.concatenate([res, x, g, jnp.zeros_like(g)], axis=0)
-        hi = full.astype(jnp.bfloat16)
-        lo = (full - hi.astype(jnp.float32)).astype(jnp.bfloat16)
-        o = jnp.dot(wcat[...], hi, preferred_element_type=jnp.float32)
-        o2 = jnp.dot(wcat[0:order, :], lo, preferred_element_type=jnp.float32)
-        new = x + (o[0:order] + (o[order:] + o2))
-        S[dst, j + 1] = new
-        if e + 1 < SWEEPS:
-            put_plane(e + 1, j, new)
+        return halves(jnp.concatenate([res, x, g, jnp.zeros_like(g)], axis=0))
 
     def do_chunk(e, c):
         if e == 0:
             take_rest(c)
         j0 = c * CHUNK
-
-        def rows(t, carry):
-            sweep_row(e, j0 + 2 * t)
-            sweep_row(e, j0 + 2 * t + 1)
-            return carry
-
-        lax.fori_loop(0, CHUNK // 2, rows, 0)
+        src, dst = S[e % 2], S[(e + 1) % 2]
+        pairs = [right_hand(e, j0 + t) for t in range(CHUNK)]
+        news = []
+        for t in range(CHUNK):
+            hi, lo = pairs[t]
+            o = jnp.dot(wcat[...], hi, preferred_element_type=jnp.float32)
+            o2 = jnp.dot(wcat[0:order, :], lo, preferred_element_type=jnp.float32)
+            news.append(src[j0 + t + 1] + (o[0:order] + (o[order:] + o2)))
+        for t in range(CHUNK):
+            dst[j0 + t + 1] = news[t]
+            if e + 1 < SWEEPS:
+                put_plane(e + 1, j0 + t, news[t])
         if e + 1 < SWEEPS:
             sister(e + 1, c).start()
         else:
@@ -271,47 +272,72 @@
             def group(g, carry):
                 gr = pl.ds(pl.multiple_of(g * 8, 8), 8)
                 xs[gr, pl.ds(j0, CHUNK), :] = jnp.swapaxes(
-                    S[(e + 1) % 2, pl.ds(j0 + 1, CHUNK), gr, :], 0, 1
+                    dst[pl.ds(j0 + 1, CHUNK), gr, :], 0, 1
                 )
                 return carry
 
-            lax.fori_loop(0, order // 8, group, 0)
+            lax.fori_loop(0, order // 8, group, 0, unroll=6)
             store(c).start()
 
     def ghost_row(e, f):
         picked = recv[e, 0, 1 - f]
         for bit in range(1, BITS):
             picked = jnp.where(pbit[0, 0] == bit, recv[e, bit, 1 - f], picked)
-        picked = jnp.dot(picked, turn_k[...], precision=EXACT, preferred_element_type=jnp.float32)
-        picked = jnp.dot(turn_i[...], picked, precision=EXACT, preferred_element_type=jnp.float32)
-        S[e % 2, 0 if f == 0 else nj + 1] = picked
+        both = jnp.concatenate(halves(picked), axis=0)
+        both = jnp.dot(both, turn_k[...], preferred_element_type=jnp.float32)
+        parts = both.astype(jnp.bfloat16)
+        swap = turn_i[...]
+        first = jnp.dot(swap, parts[0:order], preferred_element_type=jnp.float32)
+        second = jnp.dot(swap, parts[order:], preferred_element_type=jnp.float32)
+        S[e % 2][0 if f == 0 else nj + 1] = first + second
 
     for e in range(SWEEPS):
         sister(e, 1).wait_recv()
         sister(e, 2).wait_recv()
 
-        def inner(c, carry):
-            sister(e, c + 1).wait_recv()
+        def step(pos, carry):
+            c = jnp.where(
+                pos < nch - 4,
+                pos + 2,
+                jnp.where(
+                    pos < nch - 2,
+                    1 + (pos - (nch - 4)) * (nch - 3),
+                    (pos - (nch - 2)) * (nch - 1),
+                ),
+            )
+
+            @pl.when(pos < nch - 4)
+            def _():
+                sister(e, pos + 3).wait_recv()
+
+            @pl.when(pos == nch - 4)
+            def _():
+                sister(e, 0).wait_recv()
+
+            @pl.when(pos == nch - 3)
+            def _():
+                sister(e, nch - 1).wait_recv()
+
+            @pl.when(pos == nch - 2)
+            def _():
+                for f in range(2):
+                    for bit in range(BITS):
+                        face(e, bit, f).wait()
+                    edge(e, f).wait()
+                for f in range(2):
+                    ghost_row(e, f)
+
             do_chunk(e, c)
+            if e + 1 < SWEEPS:
+                for f in range(2):
+
+                    @pl.when(pos == nch - 2 + f)
+                    def _():
+                        send_ends(e + 1, f)
+
             return carry
 
-        lax.fori_loop(2, nch - 2, inner, 0)
-        sister(e, 0).wait_recv()
-        do_chunk(e, 1)
-        sister(e, nch - 1).wait_recv()
-        do_chunk(e, nch - 2)
-        for bit in range(BITS):
-            for f in range(2):
-                face(e, bit, f).wait()
-        for f in range(2):
-            edge(e, f).wait()
-            ghost_row(e, f)
-        do_chunk(e, 0)
-        if e + 1 < SWEEPS:
-            send_ends(e + 1, 0)
-        do_chunk(e, nch - 1)
-        if e + 1 < SWEEPS:
-            send_ends(e + 1, 1)
+        lax.fori_loop(0, nch, step, 0)
 
         def sent(c, carry):
             sister(e, c).wait_send()
@@ -341,7 +367,8 @@
         in_specs=[anywhere] * 3 + [smem, vmem, smem, smem, smem, smem],
         out_specs=anywhere,
         scratch_shapes=[
-            pltpu.VMEM((2, nj + 2, order, nk), f32),
+            pltpu.VMEM((nj + 2, order, nk), f32),
+            pltpu.VMEM((nj + 2, order, nk), f32),
             pltpu.VMEM((nj, order, nk), f32),
             pltpu.VMEM((nj, ni, nk), f32),
             pltpu.VMEM((order, nj, nk), f32),
@@ -351,8 +378,8 @@
             pltpu.VMEM((SWEEPS, nj + 2 * HW, 8, nk), f32),
             pltpu.VMEM((SWEEPS, nj, 8, nk), f32),
             pltpu.VMEM((2 * order, 2 * order + 16), jnp.bfloat16),
-            pltpu.VMEM((order, order), f32),
-            pltpu.VMEM((nk, nk), f32),
+            pltpu.VMEM((order, order), jnp.bfloat16),
+            pltpu.VMEM((nk, nk), jnp.bfloat16),
             pltpu.SMEM((nj, 2 * HW + 1), f32),
             dma((3, nch)),
             dma((nch,)),
@@ -375,10 +402,10 @@
         state.reshape(order, nj, nk),
         forcing.reshape(order, nj, nk),
         stiffness.reshape(ni, nj, nk),
-        advection[0, 0],
+        advection.transpose(0, 2, 1, 3)[0],
         inverse[0, 0],
-        mrows[0, 0],
-        mweights[0, 0],
+        mrows[0, 0].T,
+        mweights[0, 0].T,
         pbit,
         tcode,
     )

time: 71.4 us -> 47.3 us (0.66)
  Pallas kernels: 59.4 us -> 39.4 us
  local copies, waits for them, and re-layouts: 10.3 us -> 6.3 us
    pallas_call x1, Pallas kernels: 59.4 us -> 39.4 us  [body(): pl.pallas_call(functools.partial(kernel, nblk, nv, ni), out_shape=jax.Sha...]
    unnamed x4 -> x1, local copies, waits for them, and re-layouts: 10.3 us -> 6.3 us
where the time goes in v1:
time: 47.3 us; the launch traced here: 47 us
  Pallas kernels  39.4 us (83%)
  local copies, waits for them, and re-layouts  6.3 us (13%)
  between operations  1.3 us (3%)
    pallas_call x1, Pallas kernels, body(): pl.pallas_call(functools.partial(kernel, nblk, nv, ni), out_shape=jax.Sha...  39.4 us
    unnamed x1, local copies, waits for them, and re-layouts  6.3 us

profile of v1, /device:TPU:0, one launch (start us, length us, event | category | flops | bytes accessed | tf_op | source)
XLA Modules:
  0.0 47.0 jit_solution(4805621527376545850)
XLA Ops:
  1.3 39.4 %shard_map.91 = f32[96,64,256]{2,1,0:T(8,128)} custom-call(f32[96,64,256]{2,1,0:T(8,128)} %bitcast.13, f32[96,64,256]{2,1,0:T(8,128)} %bitcast.14, f32[16,64,256]{2,1,0:T(8,128)} %bitcast.15, f32[6,1,6]{2,1,0:T(1,128)} %bitcast.17, f32[96,96]{1,0:T(8,128)} %bitcast.16, s32[4,64]{1,0:T(4,128)} %bitcast.18, f32[4,64]{1,0:T(4,128)} %bitcast.19, ...), custom_call_target="tpu_custom_call" | custom-call | flops 5888802816 | bytes 19922944 | tf_op jit(solution)/shard_map/pallas_call | solution.py:364
  40.7 6.3 %copy.13 = f32[1,1,6,16,64,256]{5,4,3,2,1,0:T(8,128)} copy(f32[1,1,6,16,64,256]{5,4,3,2,1,0:T(8,128)} %bitcast.12) | data formatting | bytes 12582912

commit v2 on v1

--- a/solution.py
+++ b/solution.py
@@ -74,6 +74,10 @@
     turn_i,
     turn_k,
     coef,
+    RH0,
+    RH1,
+    RL0,
+    RL1,
     in_sem,
     out_sem,
     face_send,
@@ -84,7 +88,7 @@
     edge_recv,
 ):
     order = nv * ni
-    S = (S0, S1)
+    S, RH, RL = (S0, S1), (RH0, RH1), (RL0, RL1)
     nj, nk = x_hbm.shape[1], x_hbm.shape[2]
     nch = nj // CHUNK
     r = lax.axis_index("row")
@@ -133,15 +137,6 @@
     chosen_k = jnp.where(code // 2 == 1, nk - 1 - rk, rk)
     turn_k[...] = jnp.where(ck == chosen_k, 1.0, 0.0).astype(jnp.bfloat16)
 
-    def coefs(j, carry):
-        for d in range(2 * HW + 1):
-            total = jnp.float32(0.0)
-            for o in range(mrows.shape[0]):
-                total = total + jnp.where(mrows[o, j] == j + d, mweights[o, j], 0.0)
-            coef[j, d] = total
-        return carry
-
-    lax.fori_loop(0, nj, coefs, 0, unroll=2)
     plane[...] = jnp.zeros_like(plane)
 
     def face(e, bit, f):
@@ -199,21 +194,6 @@
         for jj in range(CHUNK):
             put_plane(0, j0 + jj, S0[j0 + jj + 1])
 
-    def take_rest(c):
-        load(1, f_hbm, fs, c).wait()
-        load(2, d_hbm, ds, c).wait()
-        j0 = pl.multiple_of(c * CHUNK, CHUNK)
-
-        def group(g, carry):
-            gr = pl.ds(pl.multiple_of(g * 8, 8), 8)
-            F[pl.ds(j0, CHUNK), gr, :] = jnp.swapaxes(fs[gr, pl.ds(j0, CHUNK), :], 0, 1)
-            return carry
-
-        lax.fori_loop(0, order // 8, group, 0, unroll=6)
-        for g in range(ni // 8):
-            gr = pl.ds(g * 8, 8)
-            D[pl.ds(j0, CHUNK), gr, :] = jnp.swapaxes(ds[gr, pl.ds(j0, CHUNK), :], 0, 1)
-
     take_state(0)
     pl.semaphore_wait(barrier, len(friends))
     sister(0, 0).start()
@@ -229,54 +209,88 @@
 
     lax.fori_loop(1, nch - 1, middle, 0)
 
-    lane = lax.broadcasted_iota(jnp.int32, (order, nk), 1)
+    lane = lax.broadcasted_iota(jnp.int32, (order, 128), 1)
 
     def halves(value):
         hi = value.astype(jnp.bfloat16)
         return hi, (value - hi.astype(jnp.float32)).astype(jnp.bfloat16)
 
+    def span_sum(x):
+        tiles = [x[:, t : t + 128] for t in range(0, nk, 128)]
+        after = [pltpu.roll(t, 1, 1) for t in tiles]
+        ahead = [pltpu.roll(t, 127, 1) for t in tiles]
+        sums = []
+        for t in range(len(tiles)):
+            from_left = after[t - 1] if t else 0.0
+            from_right = ahead[t + 1] if t + 1 < len(tiles) else 0.0
+            below = jnp.where(lane == 0, from_left, after[t])
+            above = jnp.where(lane == 127, from_right, ahead[t])
+            sums.append(below + above)
+        return jnp.concatenate(sums, axis=1)
+
     def right_hand(e, j):
         src = S[e % 2]
         x = src[j + 1]
-        below = jnp.where(lane == 0, 0.0, pltpu.roll(x, 1, 1))
-        above = jnp.where(lane == nk - 1, 0.0, pltpu.roll(x, nk - 1, 1))
         diag = jnp.concatenate([D[j]] * nv, axis=0)
-        near = (src[j] + src[j + 2]) + (below + above)
+        near = (src[j] + src[j + 2]) + span_sum(x)
         res = F[j] - diag * x + near
-        g = coef[j, 0] * win[e, j]
-        for d in range(1, 2 * HW + 1):
-            g = g + coef[j, d] * win[e, j + d]
+        g = None
+        for d in range(2 * HW + 1):
+            if e == 0:
+                c = jnp.float32(0.0)
+                for o in range(mrows.shape[0]):
+                    c = c + jnp.where(mrows[o, j] == j + d, mweights[o, j], 0.0)
+                coef[j, d] = c
+            else:
+                c = coef[j, d]
+            term = c * win[e, j + d]
+            g = term if g is None else g + term
         return halves(jnp.concatenate([res, x, g, jnp.zeros_like(g)], axis=0))
 
-    def do_chunk(e, c):
-        if e == 0:
-            take_rest(c)
-        j0 = c * CHUNK
-        src, dst = S[e % 2], S[(e + 1) % 2]
-        pairs = [right_hand(e, j0 + t) for t in range(CHUNK)]
+    def wait_rest(c):
+        load(1, f_hbm, fs, c).wait()
+        load(2, d_hbm, ds, c).wait()
+
+    def take_rest(c):
+        rows = pl.ds(pl.multiple_of(c * CHUNK, CHUNK), CHUNK)
+        for g in range(order // 8):
+            gr = pl.ds(g * 8, 8)
+            F[rows, gr, :] = jnp.swapaxes(fs[gr, rows, :], 0, 1)
+        for g in range(ni // 8):
+            gr = pl.ds(g * 8, 8)
+            D[rows, gr, :] = jnp.swapaxes(ds[gr, rows, :], 0, 1)
+
+    def advance(now, later):
+        if later is not None and later[0] == 0:
+            take_rest(later[1])
         news = []
         for t in range(CHUNK):
-            hi, lo = pairs[t]
-            o = jnp.dot(wcat[...], hi, preferred_element_type=jnp.float32)
-            o2 = jnp.dot(wcat[0:order, :], lo, preferred_element_type=jnp.float32)
-            news.append(src[j0 + t + 1] + (o[0:order] + (o[order:] + o2)))
-        for t in range(CHUNK):
-            dst[j0 + t + 1] = news[t]
-            if e + 1 < SWEEPS:
-                put_plane(e + 1, j0 + t, news[t])
+            if later is not None:
+                e, c, slot = later
+                hi, lo = right_hand(e, c * CHUNK + t)
+                RH[slot][t] = hi
+                RL[slot][t] = lo
+            if now is not None:
+                e, c, slot = now
+                j = c * CHUNK + t
+                o = jnp.dot(wcat[...], RH[slot][t], preferred_element_type=jnp.float32)
+                o2 = jnp.dot(wcat[0:order, :], RL[slot][t], preferred_element_type=jnp.float32)
+                new = S[e % 2][j + 1] + (o[0:order] + (o[order:] + o2))
+                if e + 1 < SWEEPS:
+                    S[(e + 1) % 2][j + 1] = new
+                    put_plane(e + 1, j, new)
+                else:
+                    news.append(new)
+        if now is None:
+            return
+        e, c, slot = now
         if e + 1 < SWEEPS:
             sister(e + 1, c).start()
         else:
-            j0 = pl.multiple_of(j0, CHUNK)
-
-            def group(g, carry):
-                gr = pl.ds(pl.multiple_of(g * 8, 8), 8)
-                xs[gr, pl.ds(j0, CHUNK), :] = jnp.swapaxes(
-                    dst[pl.ds(j0 + 1, CHUNK), gr, :], 0, 1
-                )
-                return carry
-
-            lax.fori_loop(0, order // 8, group, 0, unroll=6)
+            rows = pl.ds(pl.multiple_of(c * CHUNK, CHUNK), CHUNK)
+            for g in range(0, order, 8):
+                block = jnp.stack([new[g : g + 8] for new in news])
+                xs[g : g + 8, rows, :] = jnp.swapaxes(block, 0, 1)
             store(c).start()
 
     def ghost_row(e, f):
@@ -291,53 +305,66 @@
         second = jnp.dot(swap, parts[order:], preferred_element_type=jnp.float32)
         S[e % 2][0 if f == 0 else nj + 1] = first + second
 
+    def chunk_at(pos):
+        return jnp.where(
+            pos < nch - 4,
+            pos + 2,
+            jnp.where(pos < nch - 3, 1, jnp.where(pos < nch - 2, nch - 2, 0)),
+        )
+
+    def ready(e, pos):
+        @pl.when(pos < nch - 4)
+        def _():
+            sister(e, pos + 3).wait_recv()
+
+        @pl.when(pos == nch - 4)
+        def _():
+            sister(e, 0).wait_recv()
+
+        @pl.when(pos == nch - 3)
+        def _():
+            sister(e, nch - 1).wait_recv()
+
+        @pl.when(pos == nch - 2)
+        def _():
+            for f in range(2):
+                for bit in range(BITS):
+                    face(e, bit, f).wait()
+                edge(e, f).wait()
+            for f in range(2):
+                ghost_row(e, f)
+
+        if e == 0:
+            wait_rest(chunk_at(pos))
+
+    def first_ready(e):
+        for c in (1, 2, 3):
+            sister(e, c).wait_recv()
+        if e == 0:
+            wait_rest(2)
+
+    first_ready(0)
+    advance(None, (0, 2, 0))
     for e in range(SWEEPS):
-        sister(e, 1).wait_recv()
-        sister(e, 2).wait_recv()
-
-        def step(pos, carry):
-            c = jnp.where(
-                pos < nch - 4,
-                pos + 2,
-                jnp.where(
-                    pos < nch - 2,
-                    1 + (pos - (nch - 4)) * (nch - 3),
-                    (pos - (nch - 2)) * (nch - 1),
-                ),
-            )
-
-            @pl.when(pos < nch - 4)
-            def _():
-                sister(e, pos + 3).wait_recv()
-
-            @pl.when(pos == nch - 4)
-            def _():
-                sister(e, 0).wait_recv()
-
-            @pl.when(pos == nch - 3)
-            def _():
-                sister(e, nch - 1).wait_recv()
-
-            @pl.when(pos == nch - 2)
-            def _():
-                for f in range(2):
-                    for bit in range(BITS):
-                        face(e, bit, f).wait()
-                    edge(e, f).wait()
-                for f in range(2):
-                    ghost_row(e, f)
-
-            do_chunk(e, c)
-            if e + 1 < SWEEPS:
-                for f in range(2):
-
-                    @pl.when(pos == nch - 2 + f)
-                    def _():
-                        send_ends(e + 1, f)
-
+
+        def two(it, carry):
+            for half in range(2):
+                pos = 2 * it + half
+                ready(e, pos + 1)
+                advance((e, chunk_at(pos), half), (e, chunk_at(pos + 1), 1 - half))
             return carry
 
-        lax.fori_loop(0, nch, step, 0)
+        lax.fori_loop(0, nch // 2 - 1, two, 0)
+        if e == 0:
+            wait_rest(nch - 1)
+        advance((e, 0, 0), (e, nch - 1, 1))
+        if e + 1 < SWEEPS:
+            send_ends(e + 1, 0)
+            first_ready(e + 1)
+            advance((e, nch - 1, 1), (e + 1, 2, 0))
+            send_ends(e + 1, 1)
+        else:
+            advance((e, nch - 1, 1), None)
 
         def sent(c, carry):
             sister(e, c).wait_send()
@@ -381,6 +408,9 @@
             pltpu.VMEM((order, order), jnp.bfloat16),
             pltpu.VMEM((nk, nk), jnp.bfloat16),
             pltpu.SMEM((nj, 2 * HW + 1), f32),
+        ]
+        + [pltpu.VMEM((CHUNK, 2 * order + 16, nk), jnp.bfloat16)] * 4
+        + [
             dma((3, nch)),
             dma((nch,)),
             dma((SWEEPS, BITS, 2)),

time: 47.3 us -> 47.6 us (level)
  no operation moved by 1% of the time
where the time goes in v2:
time: 47.6 us; the launch traced here: 47.4 us
  Pallas kernels  39.8 us (84%)
  local copies, waits for them, and re-layouts  6.3 us (13%)
  between operations  1.3 us (3%)
    pallas_call x1, Pallas kernels, body(): pl.pallas_call(functools.partial(kernel, nblk, nv, ni), out_shape=jax.Sha...  39.8 us
    unnamed x1, local copies, waits for them, and re-layouts  6.3 us

profile of v2, /device:TPU:0, one launch (start us, length us, event | category | flops | bytes accessed | tf_op | source)
XLA Modules:
  0.0 47.4 jit_solution(2557070521734644805)
XLA Ops:
  1.3 39.8 %shard_map.91 = f32[96,64,256]{2,1,0:T(8,128)} custom-call(f32[96,64,256]{2,1,0:T(8,128)} %bitcast.13, f32[96,64,256]{2,1,0:T(8,128)} %bitcast.14, f32[16,64,256]{2,1,0:T(8,128)} %bitcast.15, f32[6,1,6]{2,1,0:T(1,128)} %bitcast.17, f32[96,96]{1,0:T(8,128)} %bitcast.16, s32[4,64]{1,0:T(4,128)} %bitcast.18, f32[4,64]{1,0:T(4,128)} %bitcast.19, ...), custom_call_target="tpu_custom_call" | custom-call | flops 5888802816 | bytes 19922944 | tf_op jit(solution)/shard_map/pallas_call | solution.py:391
  41.1 6.3 %copy.13 = f32[1,1,6,16,64,256]{5,4,3,2,1,0:T(8,128)} copy(f32[1,1,6,16,64,256]{5,4,3,2,1,0:T(8,128)} %bitcast.12) | data formatting | bytes 12582912

commit v3 on v2

--- a/solution.py
+++ b/solution.py
@@ -139,10 +139,11 @@
 
     plane[...] = jnp.zeros_like(plane)
 
-    def face(e, bit, f):
+    def face(e, bit, f, first=0, count=None):
+        lines = pl.ds(first, order if count is None else count)
         return pltpu.make_async_remote_copy(
-            src_ref=S[e % 2].at[1 if f == 0 else nj],
-            dst_ref=recv.at[e, bit, f],
+            src_ref=S[e % 2].at[1 if f == 0 else nj, lines],
+            dst_ref=recv.at[e, bit, f, lines],
             send_sem=face_send.at[e, bit, f],
             recv_sem=face_recv.at[e, bit, f],
             device_id=(r, partners[bit]),
@@ -176,9 +177,10 @@
             plane[e, j, v : v + 1, :] = jnp.where(rotor, last, first)
 
     def send_ends(e, f):
-        for bit in range(BITS):
-            face(e, bit, f).start()
         edge(e, 1 - f).start()
+        for first in range(0, order, 24):
+            for bit in range(BITS):
+                face(e, bit, f, first, 24).start()
 
     def take_state(c):
         load(0, x_hbm, xs, c).wait()

time: 47.6 us -> 45.9 us (0.964)
  Pallas kernels: 39.8 us -> 38.1 us
    pallas_call x1, Pallas kernels: 39.8 us -> 38.1 us  [body(): pl.pallas_call(functools.partial(kernel, nblk, nv, ni), out_shape=jax.Sha...]
where the time goes in v3:
time: 45.9 us; the launch traced here: 45.7 us
  Pallas kernels  38.1 us (83%)
  local copies, waits for them, and re-layouts  6.3 us (14%)
  between operations  1.3 us (3%)
    pallas_call x1, Pallas kernels, body(): pl.pallas_call(functools.partial(kernel, nblk, nv, ni), out_shape=jax.Sha...  38.1 us
    unnamed x1, local copies, waits for them, and re-layouts  6.3 us

profile of v3, /device:TPU:0, one launch (start us, length us, event | category | flops | bytes accessed | tf_op | source)
XLA Modules:
  0.0 45.7 jit_solution(13736341453614193603)
XLA Ops:
  1.3 38.1 %shard_map.91 = f32[96,64,256]{2,1,0:T(8,128)} custom-call(f32[96,64,256]{2,1,0:T(8,128)} %bitcast.13, f32[96,64,256]{2,1,0:T(8,128)} %bitcast.14, f32[16,64,256]{2,1,0:T(8,128)} %bitcast.15, f32[6,1,6]{2,1,0:T(1,128)} %bitcast.17, f32[96,96]{1,0:T(8,128)} %bitcast.16, s32[4,64]{1,0:T(4,128)} %bitcast.18, f32[4,64]{1,0:T(4,128)} %bitcast.19, ...), custom_call_target="tpu_custom_call" | custom-call | flops 5888802816 | bytes 19922944 | tf_op jit(solution)/shard_map/pallas_call | solution.py:393
  39.4 6.3 %copy.13 = f32[1,1,6,16,64,256]{5,4,3,2,1,0:T(8,128)} copy(f32[1,1,6,16,64,256]{5,4,3,2,1,0:T(8,128)} %bitcast.12) | data formatting | bytes 12582912

commit v4 on v3

--- a/solution.py
+++ b/solution.py
@@ -107,8 +107,8 @@
         return pltpu.make_async_copy(src.at[:, rows, :], dst.at[:, rows, :], in_sem.at[which, c])
 
     def store(c):
-        rows = pl.ds(pl.multiple_of(c * CHUNK, CHUNK), CHUNK)
-        return pltpu.make_async_copy(xs.at[:, rows, :], out_hbm.at[:, rows, :], out_sem.at[c])
+        lines = S[SWEEPS % 2].at[pl.ds(c * CHUNK + 1, CHUNK)]
+        return pltpu.make_async_copy(lines, out_hbm.at[pl.ds(c * CHUNK, CHUNK)], out_sem.at[c])
 
     for c in [0, nch - 1] + list(range(1, nch - 1)):
         load(0, x_hbm, xs, c).start()
@@ -265,7 +265,6 @@
     def advance(now, later):
         if later is not None and later[0] == 0:
             take_rest(later[1])
-        news = []
         for t in range(CHUNK):
             if later is not None:
                 e, c, slot = later
@@ -278,21 +277,15 @@
                 o = jnp.dot(wcat[...], RH[slot][t], preferred_element_type=jnp.float32)
                 o2 = jnp.dot(wcat[0:order, :], RL[slot][t], preferred_element_type=jnp.float32)
                 new = S[e % 2][j + 1] + (o[0:order] + (o[order:] + o2))
+                S[(e + 1) % 2][j + 1] = new
                 if e + 1 < SWEEPS:
-                    S[(e + 1) % 2][j + 1] = new
                     put_plane(e + 1, j, new)
-                else:
-                    news.append(new)
         if now is None:
             return
         e, c, slot = now
         if e + 1 < SWEEPS:
             sister(e + 1, c).start()
         else:
-            rows = pl.ds(pl.multiple_of(c * CHUNK, CHUNK), CHUNK)
-            for g in range(0, order, 8):
-                block = jnp.stack([new[g : g + 8] for new in news])
-                xs[g : g + 8, rows, :] = jnp.swapaxes(block, 0, 1)
             store(c).start()
 
     def ghost_row(e, f):
@@ -381,6 +374,11 @@
     lax.fori_loop(0, nch, finish, 0)
 
 
+def lines_to_cells(lines, cells):
+    for g in range(0, lines.shape[1], 8):
+        cells[g : g + 8] = jnp.swapaxes(lines[:, g : g + 8, :], 0, 1)
+
+
 def body(nblk, state, forcing, stiffness, advection, inverse, mrows, mweights, pbit, tcode):
     _, _, nv, ni, nj, nk = state.shape
     order = nv * ni
@@ -392,7 +390,7 @@
     dma = pltpu.SemaphoreType.DMA
     out = pl.pallas_call(
         functools.partial(kernel, nblk, nv, ni),
-        out_shape=jax.ShapeDtypeStruct((order, nj, nk), f32),
+        out_shape=jax.ShapeDtypeStruct((nj, order, nk), f32),
         in_specs=[anywhere] * 3 + [smem, vmem, smem, smem, smem, smem],
         out_specs=anywhere,
         scratch_shapes=[
@@ -441,6 +439,17 @@
         pbit,
         tcode,
     )
+    out = pl.pallas_call(
+        lines_to_cells,
+        grid=(nch,),
+        out_shape=jax.ShapeDtypeStruct((order, nj, nk), f32),
+        in_specs=[pl.BlockSpec((CHUNK, order, nk), lambda c: (c, 0, 0))],
+        out_specs=pl.BlockSpec((order, CHUNK, nk), lambda c: (0, c, 0)),
+        compiler_params=pltpu.CompilerParams(vmem_limit_bytes=60 * 1024 * 1024),
+        cost_estimate=pl.CostEstimate(
+            flops=0, bytes_accessed=8 * order * nj * nk, transcendentals=0
+        ),
+    )(out)
     return out.reshape(state.shape)
 
 

time: 45.9 us -> 47.5 us (1.035)
  Pallas kernels: 38.1 us -> 45.8 us
  local copies, waits for them, and re-layouts: 6.3 us -> 0 us
    pallas_call x0 -> x1, Pallas kernels: none -> 8.15 us  [body(): pl.pallas_call(lines_to_cells, grid=(nch,), out_shape=jax.ShapeDtypeStruc...]
    unnamed x1 -> x0, local copies, waits for them, and re-layouts: 6.3 us -> none
where the time goes in v4:
time: 47.5 us; the launch traced here: 47.1 us
  Pallas kernels  45.8 us (96%)
  between operations  1.3 us (3%)
    pallas_call x1, Pallas kernels, body(): pl.pallas_call(functools.partial(kernel, nblk, nv, ni), out_shape=jax.Sha...  37.6 us
    pallas_call x1, Pallas kernels, body(): pl.pallas_call(lines_to_cells, grid=(nch,), out_shape=jax.ShapeDtypeStruc...  8.15 us

profile of v4, /device:TPU:0, one launch (start us, length us, event | category | flops | bytes accessed | tf_op | source)
XLA Modules:
  0.0 47.1 jit_solution(3470789610469667367)
XLA Ops:
  1.3 37.6 %shard_map.91.lines = f32[64,96,256]{2,1,0:T(8,128)} custom-call(f32[96,64,256]{2,1,0:T(8,128)} %bitcast.12, f32[96,64,256]{2,1,0:T(8,128)} %bitcast.13, f32[16,64,256]{2,1,0:T(8,128)} %bitcast.14, f32[6,1,6]{2,1,0:T(1,128)} %bitcast.16, f32[96,96]{1,0:T(8,128)} %bitcast.15, s32[4,64]{1,0:T(4,128)} %bitcast.17, f32[4,64]{1,0:T(4,128)} %bitcast.18, ...), custom_call_target="tpu_custom_call" | custom-call | flops 5888802816 | bytes 19922944 | tf_op jit(solution)/shard_map/pallas_call | solution.py:391
  38.9 8.1 %shard_map.92 = f32[96,64,256]{2,1,0:T(8,128)} custom-call(f32[64,96,256]{2,1,0:T(8,128)} %shard_map.91.lines), custom_call_target="tpu_custom_call" | custom-call | bytes 12582912 | tf_op jit(solution)/shard_map/pallas_call | solution.py:442
